TPU v7x, 32 devices: a whole 2x2x4 slice. The times are simulated.
32 devices in a mesh: dp: 8 (over z, x), space: 4 (over y, core).
Axes of the slice: x: 2, y: 2, z: 4, core: 2. Of those that a mesh axis runs over, the one named last changes fastest.
Arguments:
- volume: bfloat16 [8, 4, 16, 8, 512], P('dp', None, 'space'), may hold values from -6 to 6
- cotangent: bfloat16 [8, 32, 4, 2, 128], P('dp', None, 'space'), may hold values from -1 to 1
- w_first: bfloat16 [16, 4, 3, 3, 3], replicated, may hold values from -0.625 to 0.625
- b_first: float32 [16], replicated, may hold values from -3 to 3
- w_second: bfloat16 [32, 16, 3, 3, 3], replicated, may hold values from -0.3125 to 0.3125
- b_second: float32 [32], replicated, may hold values from -3 to 3
Outputs:
- output: bfloat16 [8, 32, 4, 2, 128], P('dp', None, 'space')
- grad_w_first: float32 [16, 4, 3, 3, 3], replicated
- grad_b_first: float32 [16], replicated
- grad_w_second: float32 [32, 16, 3, 3, 3], replicated
- grad_b_second: float32 [32], replicated
All inputs are finite; a program needn't handle non-finite values.
Results may differ from a plain program's by a relative error of at most 0.0047.
Values may be sent and summed in bfloat16 or wider, within the bound.
A program may use at most 128 MiB of HBM per device.

v0:
```python
import functools

import jax
import jax.numpy as jnp
import ml_dtypes
import numpy as np
from jax import lax
from jax.experimental import pallas as pl
from jax.experimental.pallas import tpu as pltpu
from jax.sharding import PartitionSpec as P

F32, BF16 = jnp.float32, jnp.bfloat16
MESH = pl.DeviceIdType.MESH
TILES = 16
EARLY = 14


def dot(a, b, over=(1, 0)):
    return lax.dot_general(a, b, (((over[0],), (over[1],)), ((), ())), preferred_element_type=F32)


def sigmoid(v):
    return 0.5 * jnp.tanh(0.5 * v) + 0.5


def lanes(rows, width=128):
    return lax.broadcasted_iota(jnp.int32, (rows, width), 1)


def column(row, n):
    at = lax.broadcasted_iota(jnp.int32, (n, n), 0)
    return jnp.sum(jnp.where(at == lanes(n, n), row, 0.0), axis=1, keepdims=True)


def as_row(col, n):
    at = lax.broadcasted_iota(jnp.int32, (n, 128), 0)
    return jnp.sum(jnp.where(at == lanes(n), col, 0.0), axis=0, keepdims=True)


def spread(plane, ch, dst, base):
    lane = lanes(ch)
    zero = jnp.zeros((ch, 128), F32)
    src = {}
    for row in range(2):
        for u in range(2):
            for col in range(2):
                at = (row * 2 + col) * ch
                src[row, u, col] = plane[at : at + ch, u * 128 : u * 128 + 128].astype(F32)
            src[row, u, -1] = jnp.where(lane == 0, 0.0, pltpu.roll(src[row, u, 1], 1, 1))
            src[row, u, 2] = jnp.where(lane == 127, 0.0, pltpu.roll(src[row, u, 0], 127, 1))
    for row in range(-1, 3):
        for col in range(-1, 3):
            at = base + ((row + 1) * 4 + col + 1) * ch
            if row == -1:
                pair = (zero, src[1, 0, col])
            elif row == 2:
                pair = (src[0, 1, col], zero)
            else:
                pair = (src[row, 0, col], src[row, 1, col])
            dst[at : at + ch, 0:128] = pair[0].astype(BF16)
            dst[at : at + ch, 128:256] = pair[1].astype(BF16)


def kernel(
    nd, ns,
    vol, cot, w1, b1, w2, b2, pmat, emat, rep1, rep2, operm,
    out, gw2, gw1, gb,
    field, slope1, taps, w1t, w2t, wback, pool, poolx, phalo, grad, gradx, ghalo, fold_a, fold_b,
    sums, parts, total,
    send_sem, recv_sem, s_send, s_recv, t_send, t_recv,
):
    dp, sp = lax.axis_index("dp"), lax.axis_index("space")
    count = nd * ns
    me = dp * ns + sp
    stride = count // TILES
    has_left, has_right = sp > 0, sp < ns - 1

    def device(index):
        return (index // ns, lax.rem(index, ns))

    barrier = pltpu.get_barrier_semaphore()

    def greet(k, carry):
        pl.semaphore_signal(barrier, inc=1, device_id=device(lax.rem(me + k, count)), device_id_type=MESH)
        return carry

    lax.fori_loop(1, count, greet, 0)

    class Exchange:
        def __init__(self, slot, to_left, to_right, from_left, from_right):
            self.left = lambda: pltpu.make_async_remote_copy(
                src_ref=to_left, dst_ref=from_right, send_sem=send_sem.at[2 * slot],
                recv_sem=recv_sem.at[2 * slot], device_id=(dp, sp - 1), device_id_type=MESH)
            self.right = lambda: pltpu.make_async_remote_copy(
                src_ref=to_right, dst_ref=from_left, send_sem=send_sem.at[2 * slot + 1],
                recv_sem=recv_sem.at[2 * slot + 1], device_id=(dp, sp + 1), device_id_type=MESH)
            self.from_left, self.from_right = from_left, from_right

        def start(self):
            @pl.when(has_left)
            def _():
                self.left().start()

            @pl.when(has_right)
            def _():
                self.right().start()

        def receive(self):
            @pl.when(has_left)
            def _():
                self.right().wait_recv()

            @pl.when(has_right)
            def _():
                self.left().wait_recv()

        def clear(self):
            @pl.when(jnp.logical_not(has_left))
            def _():
                self.from_left[...] = jnp.zeros(self.from_left.shape, BF16)

            @pl.when(jnp.logical_not(has_right))
            def _():
                self.from_right[...] = jnp.zeros(self.from_right.shape, BF16)

        def finish(self):
            @pl.when(has_left)
            def _():
                self.left().wait_send()

            @pl.when(has_right)
            def _():
                self.right().wait_send()

    rows = lambda ref, at, n: ref.at[pl.ds(at, n)]
    ex_field = Exchange(0, rows(field, 144, 144), rows(field, 576, 144), rows(field, 0, 144), rows(field, 720, 144))
    ex_pool = Exchange(1, rows(pool, 0, 64), rows(pool, 64, 64), rows(phalo, 0, 64), rows(phalo, 64, 64))
    ex_grad = Exchange(2, rows(grad, 0, 128), rows(grad, 128, 128), rows(ghalo, 0, 128), rows(ghalo, 128, 128))

    phases = dot(vol[...], pmat[...])
    part = [phases[:, q * 128 : q * 128 + 128] for q in range(4)]
    lane = lanes(128)
    before = jnp.where(lane == 0, 0.0, pltpu.roll(part[3], 1, 1))
    after = jnp.where(lane == 127, 0.0, pltpu.roll(part[0], 127, 1))
    part = [before] + part + [after]
    stacked = jnp.concatenate(
        [
            jnp.concatenate(
                [part[q][(c * 4 + x) * 8 : (c * 4 + x) * 8 + 8] for q in range(6) for c in range(4)], axis=0)
            for x in range(4)
        ],
        axis=1,
    ).astype(BF16)
    blocks = dot(emat[...], stacked).astype(BF16)
    for x in range(4):
        for u in range(2):
            field[144 * (x + 1) : 144 * (x + 2), u * 128 : u * 128 + 128] = blocks[
                u * 144 : u * 144 + 144, x * 128 : x * 128 + 128]

    pl.semaphore_wait(barrier, count - 1)
    ex_field.start()
    ex_field.clear()
    ex_pool.clear()
    ex_grad.clear()

    wide = lanes(24, 256)
    rep = dot(w1[...], rep1[...])
    taps[...] = jnp.zeros(taps.shape, F32)
    for q in range(4):
        for k in range(9):
            taps[q, k, 4 * q : 4 * q + 12, :] = rep[16 * k : 16 * k + 12]
    in_q = [lax.rem(wide // 16, 4) == q for q in range(4)]
    in_r = [wide // 64 == r for r in range(4)]
    band = []
    for k in range(9):
        blk = taps[0, k]
        for q in range(1, 4):
            blk = jnp.where(in_q[q], taps[q, k], blk)
        band.append(blk)
    rows_out = []
    for a in range(3):
        for y in range(6):
            blk = jnp.zeros((24, 256), F32)
            for r in range(4):
                if 0 <= y - r <= 2:
                    blk = jnp.where(in_r[r], band[a * 3 + y - r], blk)
            rows_out.append(blk)
    w1t[...] = jnp.concatenate(rows_out, axis=0).T.astype(BF16)

    bias1 = jnp.concatenate([column(b1[...], 16)] * 16, axis=0)
    bias2 = jnp.concatenate([column(b2[...], 32)] * 8, axis=0)
    acts = {}

    def first(i):
        v = dot(w1t[...], field[144 * i : 144 * i + 432]) + bias1
        s = sigmoid(v)
        slope1[256 * i : 256 * i + 256] = 0.125 * (s * (1.0 + v * (1.0 - s)))
        acts[i] = v * s

    first(1)
    first(2)

    rep = dot(w2[...], rep2[...])
    tap = lambda a, b, e: rep[((a * 3 + b) * 3 + e) * 16 : ((a * 3 + b) * 3 + e) * 16 + 16]
    own = lanes(16, 256) // 32
    rows_out = []
    for pi in range(4):
        for pr in range(4):
            for pq in range(4):
                blk = jnp.zeros((16, 256), F32)
                for k in range(8):
                    a, b, e = pi - k // 4, pr - (k // 2) % 2, pq - k % 2
                    if 0 <= a <= 2 and 0 <= b <= 2 and 0 <= e <= 2:
                        blk = jnp.where(own == k, tap(a, b, e), blk)
                rows_out.append(blk)
    w2t[...] = jnp.concatenate(rows_out, axis=0).T.astype(BF16)
    quarter = lanes(16) // 32
    back_tap = {}
    for a in range(3):
        for b in range(3):
            for col in range(2):
                blk = jnp.zeros((16, 128), F32)
                for e in range(3):
                    blk = jnp.where(quarter == col + 2 - e, tap(a, b, e)[:, 0:128], blk)
                back_tap[a, b, col] = blk.astype(BF16)
    none = jnp.zeros((16, 128), BF16)
    for k in range(8):
        for pi in range(4):
            for pr in range(4):
                at = (pi * 4 + pr) * 128
                wback[16 * k : 16 * k + 16, at : at + 128] = back_tap.get(
                    (k // 4 + 2 - pi, (k // 2) % 2 + 2 - pr, k % 2), none)

    ex_field.receive()
    first(0)
    first(3)
    for i in range(2):
        both = acts[2 * i] + acts[2 * i + 1]
        for row in range(2):
            for col in range(2):
                blk = 0.0
                for r in range(2 * row, 2 * row + 2):
                    for q in range(2 * col, 2 * col + 2):
                        blk = blk + both[(r * 4 + q) * 16 : (r * 4 + q) * 16 + 16]
                at = 64 * i + (row * 2 + col) * 16
                pool[at : at + 16] = (blk * 0.125).astype(BF16)
    ex_pool.start()
    spread(pool[0:64], 16, poolx, 256)
    spread(pool[64:128], 16, poolx, 512)
    v = dot(w2t[:, 256:768], poolx[256:768])
    cot_cols = dot(operm[...], cot[...])
    cot_cols = jnp.concatenate([cot_cols[0:32], cot_cols[32:64]], axis=1) * 0.125
    ex_pool.receive()
    spread(phalo[0:64], 16, poolx, 0)
    spread(phalo[64:128], 16, poolx, 768)
    v = v + dot(w2t[:, 0:256], poolx[0:256]) + dot(w2t[:, 768:1024], poolx[768:1024]) + bias2
    s = sigmoid(v)
    act = v * s
    slope = s * (1.0 + v * (1.0 - s))
    out_sum, grad_sum = 0.0, 0.0
    for k in range(8):
        blk = (cot_cols * slope[32 * k : 32 * k + 32]).astype(BF16)
        grad[32 * k : 32 * k + 32] = blk
        grad_sum = grad_sum + blk.astype(F32)
        out_sum = out_sum + act[32 * k : 32 * k + 32]
    ex_grad.start()

    prod = dot(poolx[...], grad[...], (1, 1))
    packed = [jnp.zeros((16, 128), F32) for _ in range(7)]
    for a in range(3):
        for b in range(3):
            for e in range(3):
                blk = jnp.zeros((16, 256), F32)
                for k in range(8):
                    at = (((k // 4 + a) * 4 + (k // 2) % 2 + b) * 4 + k % 2 + e) * 16
                    blk = jnp.where(own == k, prod[at : at + 16], blk)
                half = blk[:, 0:128] + blk[:, 128:256]
                half = half + pltpu.roll(half, 64, 1)
                half = half + pltpu.roll(half, 32, 1)
                at = (a * 3 + b) * 3 + e
                packed[at % 7] = jnp.where(quarter == at // 7, half, packed[at % 7])
    for j in range(7):
        sums[2 * j] = packed[j][0:8]
        sums[2 * j + 1] = packed[j][8:16]

    mine = lax.div(me, stride)
    owner = lax.rem(me, stride) == 0
    early = jnp.logical_and(owner, mine < EARLY)
    late = jnp.logical_and(owner, mine >= EARLY)

    def part_copy(j):
        return pltpu.make_async_remote_copy(
            src_ref=sums.at[j], dst_ref=parts.at[me], send_sem=s_send.at[j], recv_sem=s_recv,
            device_id=device(j * stride), device_id_type=MESH)

    def send_parts(low, high):
        def step(j, carry):
            @pl.when(j * stride != me)
            def _():
                part_copy(j).start()
            return carry

        lax.fori_loop(low, high, step, 0)

    def total_copy(to, sem):
        return pltpu.make_async_remote_copy(
            src_ref=total.at[mine], dst_ref=total.at[mine], send_sem=t_send, recv_sem=t_recv.at[sem],
            device_id=device(to), device_id_type=MESH)

    def add_up(sem):
        pltpu.make_async_copy(parts.at[pl.ds(0, count - 1)], parts.at[pl.ds(0, count - 1)], s_recv).wait()
        parts[me] = sums[mine]
        total[mine] = jnp.sum(parts[...], axis=0)

        def step(k, carry):
            total_copy(lax.rem(me + k, count), sem).start()
            return carry

        lax.fori_loop(1, count, step, 0)

    def take(sem, tiles, is_mine):
        def wait(n):
            pltpu.make_async_copy(total.at[pl.ds(0, n)], total.at[pl.ds(0, n)], t_recv.at[sem]).wait()

        @pl.when(is_mine)
        def _():
            wait(tiles - 1)

        @pl.when(jnp.logical_not(is_mine))
        def _():
            wait(tiles)

    send_parts(0, EARLY)

    res = (out_sum * 0.125).astype(BF16)
    res = jnp.concatenate([res[:, 0:128], res[:, 128:256]], axis=0)
    out[...] = dot(operm[...], res, (0, 0)).astype(BF16)

    spread(grad[0:128], 32, gradx, 512)
    spread(grad[128:256], 32, gradx, 1024)
    back = dot(wback[:, 512:1536], gradx[512:1536])
    ex_grad.receive()
    spread(ghalo[0:128], 32, gradx, 0)
    spread(ghalo[128:256], 32, gradx, 1536)
    back = back + dot(wback[:, 0:512], gradx[0:512]) + dot(wback[:, 1536:2048], gradx[1536:2048])

    prod = jnp.zeros((432, 256), F32)
    bias_sum = jnp.zeros((16, 256), F32)
    for i in range(4):
        blks = []
        for r in range(4):
            for q in range(4):
                at = (((i // 2) * 2 + r // 2) * 2 + q // 2) * 16
                k = 256 * i + (r * 4 + q) * 16
                blk = (back[at : at + 16] * slope1[k : k + 16]).astype(BF16)
                bias_sum = bias_sum + blk.astype(F32)
                blks.append(blk)
        prod = prod + dot(field[144 * i : 144 * i + 432], jnp.concatenate(blks, axis=0), (1, 1))

    for a in range(3):
        for b in range(3):
            blk = jnp.zeros((24, 256), F32)
            for r in range(4):
                at = (a * 6 + r + b) * 24
                blk = jnp.where(in_r[r], prod[at : at + 24], blk)
            half = blk[:, 0:128] + blk[:, 128:256]
            fold_a[a * 3 + b] = half + pltpu.roll(half, 64, 1)
    sixteenth = lanes(12) // 16
    for k in range(9):
        blk = jnp.zeros((12, 128), F32)
        for q in range(4):
            blk = jnp.where(lax.rem(sixteenth, 4) == q, fold_a[k, 4 * q : 4 * q + 12, :], blk)
        blk = blk + pltpu.roll(blk, 32, 1)
        blk = blk + pltpu.roll(blk, 16, 1)
        fold_b[12 * k : 12 * k + 12, :] = blk
    fold_b[108:120, :] = jnp.zeros((12, 128), F32)
    blk = fold_b[0:16]
    for g in range(1, 8):
        blk = jnp.where(lanes(16) // 16 == g, fold_b[14 * g : 14 * g + 16, :], blk)
    at = lax.broadcasted_iota(jnp.int32, (16, 128), 0)
    row1 = as_row(jnp.sum(bias_sum, axis=1, keepdims=True), 16)
    row2 = as_row(jnp.sum(grad_sum, axis=1, keepdims=True), 32)
    blk = jnp.where(at == 14, row1, jnp.where(at == 15, row2, blk))
    sums[EARLY] = blk[0:8]
    sums[EARLY + 1] = blk[8:16]
    send_parts(EARLY, TILES)

    @pl.when(early)
    def _():
        add_up(0)

    @pl.when(late)
    def _():
        add_up(1)

    take(0, EARLY, early)
    for g in range(4):
        n = 112 if g < 3 else 96
        blk = total[0 : n // 8].reshape(n, 128)
        if g:
            blk = pltpu.roll(blk, 128 - 32 * g, 1)
        gw2[112 * g : 112 * g + n] = blk[:, 0:32]
    take(1, TILES - EARLY, late)
    blk = jnp.concatenate([total[EARLY], total[EARLY + 1]], axis=0)
    gb[...] = total[EARLY + 1]
    for g in range(8):
        n = 14 if g < 7 else 10
        turned = pltpu.roll(blk, 128 - 16 * g, 1) if g else blk
        gw1[14 * g : 14 * g + n] = turned[0:n, 0:16]

    ex_field.finish()
    ex_pool.finish()
    ex_grad.finish()

    def sent(j, carry):
        @pl.when(j * stride != me)
        def _():
            part_copy(j).wait_send()
        return carry

    lax.fori_loop(0, TILES, sent, 0)

    @pl.when(owner)
    def _():
        pltpu.make_async_copy(parts.at[pl.ds(0, count - 1)], parts.at[pl.ds(0, count - 1)], t_send).wait()


def tables():
    pmat = np.zeros((512, 512), np.float32)
    for z in range(512):
        pmat[z, (z % 4) * 128 + z // 4] = 1
    emat = np.zeros((2, 6, 6, 4, 6, 4, 8), np.float32)
    for u in range(2):
        for yr in range(6):
            y = 4 * u + yr - 1
            if 0 <= y < 8:
                for q in range(6):
                    for c in range(4):
                        emat[u, yr, q, c, q, c, y] = 1
    rep1 = np.tile(np.eye(16, dtype=np.float32), (1, 16))
    rep2 = np.tile(np.eye(32, dtype=np.float32), (1, 8))
    operm = np.zeros((64, 64), np.float32)
    for u in range(2):
        for o in range(32):
            operm[u * 32 + o, o * 2 + u] = 1
    return [t.astype(ml_dtypes.bfloat16) for t in (pmat, emat.reshape(288, 192), rep1, rep2, operm)]


def shards(nd, ns, volume, cotangent, w_first, b_first, w_second, b_second):
    count = nd * ns
    w1 = jnp.transpose(w_first, (2, 3, 4, 1, 0)).reshape(9, 12, 16)
    w1 = jnp.pad(w1, ((0, 0), (0, 4), (0, 0))).reshape(144, 16)
    w2 = jnp.transpose(w_second, (2, 3, 4, 1, 0)).reshape(432, 32)
    vm = pl.BlockSpec(memory_space=pltpu.VMEM)
    dma = pltpu.SemaphoreType.DMA
    out, gw2, gw1, gb = pl.pallas_call(
        functools.partial(kernel, nd, ns),
        out_shape=[
            jax.ShapeDtypeStruct((64, 128), BF16),
            jax.ShapeDtypeStruct((432, 32), F32),
            jax.ShapeDtypeStruct((108, 16), F32),
            jax.ShapeDtypeStruct((8, 128), F32),
        ],
        in_specs=[vm] * 11,
        out_specs=[vm] * 4,
        scratch_shapes=[
            pltpu.VMEM((864, 256), BF16),
            pltpu.VMEM((1024, 256), F32),
            pltpu.VMEM((4, 9, 24, 256), F32),
            pltpu.VMEM((256, 432), BF16),
            pltpu.VMEM((256, 1024), BF16),
            pltpu.VMEM((128, 2048), BF16),
            pltpu.VMEM((128, 256), BF16),
            pltpu.VMEM((1024, 256), BF16),
            pltpu.VMEM((128, 256), BF16),
            pltpu.VMEM((256, 256), BF16),
            pltpu.VMEM((2048, 256), BF16),
            pltpu.VMEM((256, 256), BF16),
            pltpu.VMEM((9, 24, 128), F32),
            pltpu.VMEM((120, 128), F32),
            pltpu.VMEM((TILES, 8, 128), F32),
            pltpu.VMEM((count, 8, 128), F32),
            pltpu.VMEM((TILES, 8, 128), F32),
            dma((6,)),
            dma((6,)),
            dma((TILES,)),
            dma,
            dma,
            dma((2,)),
        ],
        compiler_params=pltpu.CompilerParams(
            collective_id=0, has_side_effects=True, vmem_limit_bytes=48 * 1024 * 1024),
        cost_estimate=pl.CostEstimate(flops=10**9, bytes_accessed=2 * 10**6, transcendentals=3 * 10**5),
    )(
        volume.reshape(128, 512), cotangent.reshape(64, 128), w1, b_first.reshape(1, 16), w2,
        b_second.reshape(1, 32), *tables(),
    )
    grad_w1 = jnp.transpose(gw1.reshape(3, 3, 3, 4, 16), (4, 3, 0, 1, 2))
    grad_w2 = jnp.transpose(gw2.reshape(3, 3, 3, 16, 32), (4, 3, 0, 1, 2))
    return out.reshape(1, 32, 1, 2, 128), grad_w1, gb[6, :16], grad_w2, gb[7, :32]


def solution(mesh):
    placed = (
        P("dp", None, "space", None, None),
        P("dp", None, "space", None, None),
        P(),
        P(),
        P(),
        P(),
    )
    return jax.shard_map(
        functools.partial(shards, mesh.shape["dp"], mesh.shape["space"]),
        mesh=mesh,
        in_specs=placed,
        out_specs=(P("dp", None, "space", None, None), P(), P(), P(), P()),
        check_vma=False,
    )
```

profile of v0, /device:TPU:0, one launch (start us, length us, event | category | flops | bytes accessed | tf_op | source)
XLA Modules:
  0.0 37.1 jit_solution(14020802410822723744)
XLA Ops:
  0.6 0.0 copy-start
  0.6 0.8 %reshape.42 = bf16[9,12,16]{2,1,0:T(8,128)(2,1)S(1)} reshape(bf16[3,3,3,4,16]{4,3,2,1,0:T(4,128)(2,1)} %bitcast.29) | data formatting | bytes 6912 | tf_op jit(solution)/shard_map/reshape | solution.py:451
  1.4 0.0 copy-start.2
  1.5 0.0 copy-start.3
  1.5 0.0 copy-start.4
  1.5 0.0 copy-done
  1.6 0.6 %copy-done.2 = bf16[1,32,1,2,128]{4,3,2,1,0:T(2,128)(2,1)S(1)} copy-done((bf16[1,32,1,2,128]{4,3,2,1,0:T(2,128)(2,1)S(1)}, bf16[1,32,1,2,128]{4,3,2,1,0:T(2,128)(2,1)}, u32[]{:S(2)}) %copy-start.2) | copy-done | bytes 16408
  2.2 0.0 copy-done.3
  2.2 0.0 copy-done.4
  2.2 0.0 copy-start.1
  2.2 0.9 %copy-done.1 = bf16[32,16,3,3,3]{0,1,4,3,2:T(8,128)(2,1)S(1)} copy-done((bf16[32,16,3,3,3]{0,1,4,3,2:T(8,128)(2,1)S(1)}, bf16[32,16,3,3,3]{0,1,4,3,2:T(8,128)(2,1)}, u32[]{:S(2)}) %copy-start.1) | copy-done | bytes 27672
  3.1 0.0 copy-start.5
  3.1 1.0 %copy-done.5 = bf16[512,512]{1,0:T(8,128)(2,1)S(1)} copy-done((bf16[512,512]{1,0:T(8,128)(2,1)S(1)}, bf16[512,512]{1,0:T(8,128)(2,1)}, u32[]{:S(2)}) %copy-start.5) | copy-done | bytes 524312
  4.1 0.0 copy-start.6
  4.1 0.9 %copy-done.6 = bf16[288,192]{1,0:T(8,128)(2,1)S(1)} copy-done((bf16[288,192]{1,0:T(8,128)(2,1)S(1)}, bf16[288,192]{1,0:T(8,128)(2,1)}, u32[]{:S(2)}) %copy-start.6) | copy-done | bytes 110616
  5.0 0.0 copy-start.7
  5.0 0.7 %copy-done.7 = bf16[64,64]{1,0:T(8,128)(2,1)S(1)} copy-done((bf16[64,64]{1,0:T(8,128)(2,1)S(1)}, bf16[64,64]{1,0:T(8,128)(2,1)}, u32[]{:S(2)}) %copy-start.7) | copy-done | bytes 8216
  5.8 0.0 copy-start.8
  5.8 0.7 %copy-done.8 = bf16[32,256]{1,0:T(8,128)(2,1)S(1)} copy-done((bf16[32,256]{1,0:T(8,128)(2,1)S(1)}, bf16[32,256]{1,0:T(8,128)(2,1)}, u32[]{:S(2)}) %copy-start.8) | copy-done | bytes 16408
  6.5 0.0 copy-start.9
  6.5 0.7 %copy-done.9 = bf16[16,256]{1,0:T(8,128)(2,1)S(1)} copy-done((bf16[16,256]{1,0:T(8,128)(2,1)S(1)}, bf16[16,256]{1,0:T(8,128)(2,1)}, u32[]{:S(2)}) %copy-start.9) | copy-done | bytes 8216
  7.2 27.0 %shard_map.146 = (bf16[64,128]{1,0:T(8,128)(2,1)S(1)}, f32[432,32]{1,0:T(8,128)S(1)}, f32[108,16]{1,0:T(8,128)S(1)}, f32[8,128]{1,0:T(8,128)S(1)}) custom-call(bf16[128,512]{1,0:T(8,128)(2,1)S(1)} %bitcast.23, bf16[64,128]{1,0:T(8,128)(2,1)S(1)} %bitcast.25, bf16[144,16]{1,0:T(8,128)(2,1)S(1)} %bitcast.21, f32[1,16]{1,0:T(1,128)S(1)} %bitcast.26, ...), custom_call_target="tpu_custom_call" | custom-call | flops 1000000000 | bytes 2000000 | tf_op jit(solution)/shard_map/pallas_call | solution.py:456
  34.2 0.5 %slice_bitcast_fusion = f32[32]{0:T(128)} fusion(f32[8,128]{1,0:T(8,128)S(1)} %get-tuple-element.11), kind=kLoop, calls=%fused_computation | loop fusion | bytes 256 | tf_op jit(solution)/shard_map/squeeze | solution.py:500
  34.7 0.5 %slice_bitcast_fusion.1 = f32[16]{0:T(128)} fusion(f32[8,128]{1,0:T(8,128)S(1)} %get-tuple-element.11), kind=kLoop, calls=%fused_computation.1 | loop fusion | bytes 128 | tf_op jit(solution)/shard_map/squeeze | solution.py:500
  35.2 0.6 %reshape.48 = f32[3,3,3,4,16]{4,3,2,1,0:T(4,128)} reshape(f32[108,16]{1,0:T(8,128)S(1)} %get-tuple-element.10) | data formatting | bytes 13824 | tf_op jit(solution)/shard_map/reshape | solution.py:498
  35.8 0.6 %copy.20 = bf16[1,32,1,2,128]{4,3,2,1,0:T(2,128)(2,1)} copy(bf16[1,32,1,2,128]{4,3,2,1,0:T(2,128)(2,1)S(1)} %bitcast.22) | data formatting | bytes 32768
  36.4 0.7 %copy.21 = f32[32,16,3,3,3]{0,1,4,3,2:T(8,128)} copy(f32[32,16,3,3,3]{0,1,4,3,2:T(8,128)S(1)} %bitcast.20) | data formatting | bytes 110592
  (1 shorter events, 0.0 us)
Async XLA Ops:
  0.6 0.9 %copy-start = (bf16[1,4,4,8,512]{4,3,2,1,0:T(8,128)(2,1)S(1)}, bf16[1,4,4,8,512]{4,3,2,1,0:T(8,128)(2,1)}, u32[]{:S(2)}) copy-start(bf16[1,4,4,8,512]{4,3,2,1,0:T(8,128)(2,1)} %param.11) | copy-start | bytes 393220
  1.4 0.7 %copy-start.2 = (bf16[1,32,1,2,128]{4,3,2,1,0:T(2,128)(2,1)S(1)}, bf16[1,32,1,2,128]{4,3,2,1,0:T(2,128)(2,1)}, u32[]{:S(2)}) copy-start(bf16[1,32,1,2,128]{4,3,2,1,0:T(2,128)(2,1)} %param.12) | copy-start | bytes 49156
  1.5 0.7 %copy-start.3 = (f32[16]{0:T(128)S(1)}, f32[16]{0:T(128)}, u32[]{:S(2)}) copy-start(f32[16]{0:T(128)} %param.14) | copy-start | bytes 196
  1.5 0.7 %copy-start.4 = (f32[32]{0:T(128)S(1)}, f32[32]{0:T(128)}, u32[]{:S(2)}) copy-start(f32[32]{0:T(128)} %param.16) | copy-start | bytes 388
  2.2 0.9 %copy-start.1 = (bf16[32,16,3,3,3]{0,1,4,3,2:T(8,128)(2,1)S(1)}, bf16[32,16,3,3,3]{0,1,4,3,2:T(8,128)(2,1)}, u32[]{:S(2)}) copy-start(bf16[32,16,3,3,3]{0,1,4,3,2:T(8,128)(2,1)} %param.15) | copy-start | bytes 82948
  3.1 1.0 %copy-start.5 = (bf16[512,512]{1,0:T(8,128)(2,1)S(1)}, bf16[512,512]{1,0:T(8,128)(2,1)}, u32[]{:S(2)}) copy-start(bf16[512,512]{1,0:T(8,128)(2,1)} %constant.13.clone.pmat) | copy-start | bytes 1572868
  4.1 0.9 %copy-start.6 = (bf16[288,192]{1,0:T(8,128)(2,1)S(1)}, bf16[288,192]{1,0:T(8,128)(2,1)}, u32[]{:S(2)}) copy-start(bf16[288,192]{1,0:T(8,128)(2,1)} %constant.14.clone.emat) | copy-start | bytes 331780
  5.0 0.7 %copy-start.7 = (bf16[64,64]{1,0:T(8,128)(2,1)S(1)}, bf16[64,64]{1,0:T(8,128)(2,1)}, u32[]{:S(2)}) copy-start(bf16[64,64]{1,0:T(8,128)(2,1)} %constant.17.clone.operm) | copy-start | bytes 24580
  5.8 0.7 %copy-start.8 = (bf16[32,256]{1,0:T(8,128)(2,1)S(1)}, bf16[32,256]{1,0:T(8,128)(2,1)}, u32[]{:S(2)}) copy-start(bf16[32,256]{1,0:T(8,128)(2,1)} %constant.16.clone.rep2) | copy-start | bytes 49156
  6.5 0.7 %copy-start.9 = (bf16[16,256]{1,0:T(8,128)(2,1)S(1)}, bf16[16,256]{1,0:T(8,128)(2,1)}, u32[]{:S(2)}) copy-start(bf16[16,256]{1,0:T(8,128)(2,1)} %constant.15.clone.rep1) | copy-start | bytes 24580
where the time goes:
time: 37.7 us; the launch traced here: 37.1 us
  Pallas kernels  27 us (72%)
  local copies, waits for them, and re-layouts  9.45 us (25%)
  between operations  0.69 us (2%)
    pallas_call x1, Pallas kernels, shards(): pl.pallas_call(functools.partial(kernel, nd, ns), out_shape=[jax.ShapeDty...  27 us
    unnamed x22, local copies, waits for them, and re-layouts  6.96 us
    reshape x1, local copies, waits for them, and re-layouts, shards(): w1 = jnp.transpose(w_first, (2, 3, 4, 1, 0)).reshape(9, 12, 16)  0.81 us

commit v1 on v0

--- a/solution.py
+++ b/solution.py
@@ -12,6 +12,7 @@
 F32, BF16 = jnp.float32, jnp.bfloat16
 MESH = pl.DeviceIdType.MESH
 TILES = 16
+INPUTS = 11
 EARLY = 14
 
 
@@ -63,12 +64,18 @@
 
 def kernel(
     nd, ns,
-    vol, cot, w1, b1, w2, b2, pmat, emat, rep1, rep2, operm,
-    out, gw2, gw1, gb,
+    *refs,
+):
+    hbm, (out, total) = refs[:INPUTS], refs[INPUTS : INPUTS + 2]
+    held, refs = refs[INPUTS + 2 : 2 * INPUTS + 2], refs[2 * INPUTS + 2 :]
+    vol, cot, w1, b1, w2, b2, pmat, emat, rep1, rep2, operm = held
+    (
     field, slope1, taps, w1t, w2t, wback, pool, poolx, phalo, grad, gradx, ghalo, fold_a, fold_b,
-    sums, parts, total,
-    send_sem, recv_sem, s_send, s_recv, t_send, t_recv,
-):
+    w1_rows, sums, parts, load_sem, send_sem, recv_sem, s_send, s_recv, t_send, t_recv,
+    ) = refs
+    loads = [pltpu.make_async_copy(hbm[i], held[i], load_sem.at[i]) for i in range(INPUTS)]
+    for copy in loads:
+        copy.start()
     dp, sp = lax.axis_index("dp"), lax.axis_index("space")
     count = nd * ns
     me = dp * ns + sp
@@ -137,6 +144,8 @@
     ex_pool = Exchange(1, rows(pool, 0, 64), rows(pool, 64, 64), rows(phalo, 0, 64), rows(phalo, 64, 64))
     ex_grad = Exchange(2, rows(grad, 0, 128), rows(grad, 128, 128), rows(ghalo, 0, 128), rows(ghalo, 128, 128))
 
+    for copy in loads:
+        copy.wait()
     phases = dot(vol[...], pmat[...])
     part = [phases[:, q * 128 : q * 128 + 128] for q in range(4)]
     lane = lanes(128)
@@ -164,7 +173,11 @@
     ex_grad.clear()
 
     wide = lanes(24, 256)
-    rep = dot(w1[...], rep1[...])
+    w1_rows[...] = jnp.zeros(w1_rows.shape, F32)
+    for k in range(27):
+        at = 16 * (k // 3) + 4 * (k % 3)
+        w1_rows[at : at + 4, :] = w1[k].astype(F32)
+    rep = dot(w1_rows[...].astype(BF16), rep1[...])
     taps[...] = jnp.zeros(taps.shape, F32)
     for q in range(4):
         for k in range(9):
@@ -394,35 +407,41 @@
         add_up(1)
 
     take(0, EARLY, early)
+    take(1, TILES - EARLY, late)
+    ex_field.finish()
+    ex_pool.finish()
+    ex_grad.finish()
+
+    def sent(j, carry):
+        @pl.when(j * stride != me)
+        def _():
+            part_copy(j).wait_send()
+        return carry
+
+    lax.fori_loop(0, TILES, sent, 0)
+
+    @pl.when(owner)
+    def _():
+        pltpu.make_async_copy(parts.at[pl.ds(0, count - 1)], parts.at[pl.ds(0, count - 1)], t_send).wait()
+
+
+def unpack(res, total, out, gw2, gw1, gb1, gb2, rows):
+    out[...] = res[...]
     for g in range(4):
         n = 112 if g < 3 else 96
         blk = total[0 : n // 8].reshape(n, 128)
         if g:
             blk = pltpu.roll(blk, 128 - 32 * g, 1)
         gw2[112 * g : 112 * g + n] = blk[:, 0:32]
-    take(1, TILES - EARLY, late)
     blk = jnp.concatenate([total[EARLY], total[EARLY + 1]], axis=0)
-    gb[...] = total[EARLY + 1]
     for g in range(8):
         n = 14 if g < 7 else 10
         turned = pltpu.roll(blk, 128 - 16 * g, 1) if g else blk
-        gw1[14 * g : 14 * g + n] = turned[0:n, 0:16]
-
-    ex_field.finish()
-    ex_pool.finish()
-    ex_grad.finish()
-
-    def sent(j, carry):
-        @pl.when(j * stride != me)
-        def _():
-            part_copy(j).wait_send()
-        return carry
-
-    lax.fori_loop(0, TILES, sent, 0)
-
-    @pl.when(owner)
-    def _():
-        pltpu.make_async_copy(parts.at[pl.ds(0, count - 1)], parts.at[pl.ds(0, count - 1)], t_send).wait()
+        rows[14 * g : 14 * g + n] = turned[0:n]
+    for k in range(27):
+        gw1[k] = rows[4 * k : 4 * k + 4, 0:16]
+    gb1[...] = blk[14:15, 0:16]
+    gb2[...] = blk[15:16, 0:32]
 
 
 def tables():
@@ -448,22 +467,24 @@
 
 def shards(nd, ns, volume, cotangent, w_first, b_first, w_second, b_second):
     count = nd * ns
-    w1 = jnp.transpose(w_first, (2, 3, 4, 1, 0)).reshape(9, 12, 16)
-    w1 = jnp.pad(w1, ((0, 0), (0, 4), (0, 0))).reshape(144, 16)
+    w1 = jnp.transpose(w_first, (2, 3, 4, 1, 0)).reshape(27, 4, 16)
     w2 = jnp.transpose(w_second, (2, 3, 4, 1, 0)).reshape(432, 32)
     vm = pl.BlockSpec(memory_space=pltpu.VMEM)
     dma = pltpu.SemaphoreType.DMA
-    out, gw2, gw1, gb = pl.pallas_call(
+    operands = [
+        volume.reshape(128, 512), cotangent.reshape(64, 128), w1, b_first.reshape(1, 16), w2,
+        b_second.reshape(1, 32), *tables(),
+    ]
+    out, total = pl.pallas_call(
         functools.partial(kernel, nd, ns),
         out_shape=[
             jax.ShapeDtypeStruct((64, 128), BF16),
-            jax.ShapeDtypeStruct((432, 32), F32),
-            jax.ShapeDtypeStruct((108, 16), F32),
-            jax.ShapeDtypeStruct((8, 128), F32),
+            jax.ShapeDtypeStruct((TILES, 8, 128), F32),
         ],
-        in_specs=[vm] * 11,
-        out_specs=[vm] * 4,
-        scratch_shapes=[
+        in_specs=[pl.BlockSpec(memory_space=pltpu.HBM)] * INPUTS,
+        out_specs=[vm] * 2,
+        scratch_shapes=[pltpu.VMEM(a.shape, a.dtype) for a in operands]
+        + [
             pltpu.VMEM((864, 256), BF16),
             pltpu.VMEM((1024, 256), F32),
             pltpu.VMEM((4, 9, 24, 256), F32),
@@ -478,9 +499,10 @@
             pltpu.VMEM((256, 256), BF16),
             pltpu.VMEM((9, 24, 128), F32),
             pltpu.VMEM((120, 128), F32),
+            pltpu.VMEM((144, 16), F32),
             pltpu.VMEM((TILES, 8, 128), F32),
             pltpu.VMEM((count, 8, 128), F32),
-            pltpu.VMEM((TILES, 8, 128), F32),
+            dma((INPUTS,)),
             dma((6,)),
             dma((6,)),
             dma((TILES,)),
@@ -489,15 +511,26 @@
             dma((2,)),
         ],
         compiler_params=pltpu.CompilerParams(
-            collective_id=0, has_side_effects=True, vmem_limit_bytes=48 * 1024 * 1024),
+            collective_id=0, has_side_effects=True, vmem_limit_bytes=62 * 1024 * 1024),
         cost_estimate=pl.CostEstimate(flops=10**9, bytes_accessed=2 * 10**6, transcendentals=3 * 10**5),
-    )(
-        volume.reshape(128, 512), cotangent.reshape(64, 128), w1, b_first.reshape(1, 16), w2,
-        b_second.reshape(1, 32), *tables(),
-    )
+    )(*operands)
+    out, gw2, gw1, gb1, gb2 = pl.pallas_call(
+        unpack,
+        out_shape=[
+            jax.ShapeDtypeStruct((64, 128), BF16),
+            jax.ShapeDtypeStruct((432, 32), F32),
+            jax.ShapeDtypeStruct((27, 4, 16), F32),
+            jax.ShapeDtypeStruct((1, 16), F32),
+            jax.ShapeDtypeStruct((1, 32), F32),
+        ],
+        in_specs=[vm] * 2,
+        out_specs=[vm] * 5,
+        scratch_shapes=[pltpu.VMEM((112, 128), F32)],
+
+    )(out, total)
     grad_w1 = jnp.transpose(gw1.reshape(3, 3, 3, 4, 16), (4, 3, 0, 1, 2))
     grad_w2 = jnp.transpose(gw2.reshape(3, 3, 3, 16, 32), (4, 3, 0, 1, 2))
-    return out.reshape(1, 32, 1, 2, 128), grad_w1, gb[6, :16], grad_w2, gb[7, :32]
+    return out.reshape(1, 32, 1, 2, 128), grad_w1, gb1.reshape(16), grad_w2, gb2.reshape(32)
 
 
 def solution(mesh):

time: 37.7 us -> 29.8 us (0.79)
  local copies, waits for them, and re-layouts: 9.45 us -> 0 us
  Pallas kernels: 27 us -> 28.9 us
    unnamed x22 -> x0, local copies, waits for them, and re-layouts: 6.96 us -> none
    pallas_call x0 -> x1, Pallas kernels: none -> 1.69 us  [shards(): pl.pallas_call(unpack, out_shape=[jax.ShapeDtypeStruct((64, 128), BF16),...]
    reshape x2 -> x0, local copies, waits for them, and re-layouts: 1.44 us -> none  [the longest x1 0.81 us: shards(): w1 = jnp.transpose(w_first, (2, 3, 4, 1, 0)).reshape(9, 12, 16)]
    squeeze x2 -> x0, local copies, waits for them, and re-layouts: 1.03 us -> none  [the longest x1 0.51 us: shards(): gb[7, :32]]
where the time goes in v1:
time: 29.8 us; the launch traced here: 29.6 us
  Pallas kernels  28.9 us (97%)
  between operations  0.64 us (2%)
    pallas_call x1, Pallas kernels, shards(): pl.pallas_call(functools.partial(kernel, nd, ns), out_shape=[jax.ShapeDty...  27.2 us
    pallas_call x1, Pallas kernels, shards(): pl.pallas_call(unpack, out_shape=[jax.ShapeDtypeStruct((64, 128), BF16),...  1.69 us

profile of v1, /device:TPU:0, one launch (start us, length us, event | category | flops | bytes accessed | tf_op | source)
XLA Modules:
  0.0 29.6 jit_solution(12561731659565319595)
XLA Ops:
  0.6 27.2 %shard_map.146 = (bf16[64,128]{1,0:T(8,128)(2,1)}, f32[16,8,128]{2,1,0:T(8,128)}) custom-call(bf16[128,512]{1,0:T(8,128)(2,1)} %bitcast.22, bf16[64,128]{1,0:T(8,128)(2,1)} %bitcast.26, bf16[27,4,16]{2,1,0:T(4,128)(2,1)} %bitcast.25, f32[1,16]{1,0:T(1,128)} %bitcast.28, bf16[432,32]{1,0:T(8,128)(2,1)} %bitcast.23, f32[1,32]{1,0:T(1,128)} %bitcast.29, ...), custom_call_target="tpu_custom_call" | custom-call | flops 1000000000 | bytes 2000000 | tf_op jit(solution)/shard_map/pallas_call | solution.py:478
  27.9 1.7 %shard_map.147 = (bf16[64,128]{1,0:T(8,128)(2,1)}, f32[432,32]{1,0:T(8,128)}, f32[27,4,16]{2,1,0:T(4,128)}, f32[1,16]{1,0:T(1,128)}, f32[1,32]{1,0:T(1,128)}) custom-call(bf16[64,128]{1,0:T(8,128)(2,1)} %get-tuple-element.12.res, f32[16,8,128]{2,1,0:T(8,128)} %get-tuple-element.13.total), custom_call_target="tpu_custom_call" | custom-call | tf_op jit(solution)/shard_map/pallas_call | solution.py:517

commit v2 on v1

--- a/solution.py
+++ b/solution.py
@@ -11,9 +11,8 @@
 
 F32, BF16 = jnp.float32, jnp.bfloat16
 MESH = pl.DeviceIdType.MESH
-TILES = 16
 INPUTS = 11
-EARLY = 14
+EARLY, LATE = 128, 16
 
 
 def dot(a, b, over=(1, 0)):
@@ -66,32 +65,35 @@
     nd, ns,
     *refs,
 ):
-    hbm, (out, total) = refs[:INPUTS], refs[INPUTS : INPUTS + 2]
-    held, refs = refs[INPUTS + 2 : 2 * INPUTS + 2], refs[2 * INPUTS + 2 :]
+    hbm, (out, total, late) = refs[:INPUTS], refs[INPUTS : INPUTS + 3]
+    held, refs = refs[INPUTS + 3 : 2 * INPUTS + 3], refs[2 * INPUTS + 3 :]
     vol, cot, w1, b1, w2, b2, pmat, emat, rep1, rep2, operm = held
     (
     field, slope1, taps, w1t, w2t, wback, pool, poolx, phalo, grad, gradx, ghalo, fold_a, fold_b,
-    w1_rows, sums, parts, load_sem, send_sem, recv_sem, s_send, s_recv, t_send, t_recv,
+    w1_rows, sums, near, far, late_near, late_far, load_sem, send_sem, recv_sem, near_sem, far_sem,
     ) = refs
+    dp, sp = lax.axis_index("dp"), lax.axis_index("space")
+    has_left, has_right = sp > 0, sp < ns - 1
+
+    barrier = pltpu.get_barrier_semaphore()
+
+    def beside(k):
+        return (dp, lax.rem(sp + k, ns))
+
+    def across(k):
+        return (lax.rem(dp + k, nd), sp)
+
+    def greet(target):
+        def step(k, carry):
+            pl.semaphore_signal(barrier, inc=1, device_id=target(k), device_id_type=MESH)
+            return carry
+        return step
+
+    lax.fori_loop(1, ns, greet(beside), 0)
+    lax.fori_loop(1, nd, greet(across), 0)
     loads = [pltpu.make_async_copy(hbm[i], held[i], load_sem.at[i]) for i in range(INPUTS)]
     for copy in loads:
         copy.start()
-    dp, sp = lax.axis_index("dp"), lax.axis_index("space")
-    count = nd * ns
-    me = dp * ns + sp
-    stride = count // TILES
-    has_left, has_right = sp > 0, sp < ns - 1
-
-    def device(index):
-        return (index // ns, lax.rem(index, ns))
-
-    barrier = pltpu.get_barrier_semaphore()
-
-    def greet(k, carry):
-        pl.semaphore_signal(barrier, inc=1, device_id=device(lax.rem(me + k, count)), device_id_type=MESH)
-        return carry
-
-    lax.fori_loop(1, count, greet, 0)
 
     class Exchange:
         def __init__(self, slot, to_left, to_right, from_left, from_right):
@@ -144,8 +146,9 @@
     ex_pool = Exchange(1, rows(pool, 0, 64), rows(pool, 64, 64), rows(phalo, 0, 64), rows(phalo, 64, 64))
     ex_grad = Exchange(2, rows(grad, 0, 128), rows(grad, 128, 128), rows(ghalo, 0, 128), rows(ghalo, 128, 128))
 
-    for copy in loads:
-        copy.wait()
+    first_used = (0, 6, 7)
+    for i in first_used:
+        loads[i].wait()
     phases = dot(vol[...], pmat[...])
     part = [phases[:, q * 128 : q * 128 + 128] for q in range(4)]
     lane = lanes(128)
@@ -166,11 +169,15 @@
             field[144 * (x + 1) : 144 * (x + 2), u * 128 : u * 128 + 128] = blocks[
                 u * 144 : u * 144 + 144, x * 128 : x * 128 + 128]
 
-    pl.semaphore_wait(barrier, count - 1)
+    pl.semaphore_wait(barrier, ns + nd - 2)
     ex_field.start()
     ex_field.clear()
     ex_pool.clear()
     ex_grad.clear()
+
+    for i in range(INPUTS):
+        if i not in first_used:
+            loads[i].wait()
 
     wide = lanes(24, 256)
     w1_rows[...] = jnp.zeros(w1_rows.shape, F32)
@@ -292,58 +299,43 @@
                 half = half + pltpu.roll(half, 32, 1)
                 at = (a * 3 + b) * 3 + e
                 packed[at % 7] = jnp.where(quarter == at // 7, half, packed[at % 7])
-    for j in range(7):
-        sums[2 * j] = packed[j][0:8]
-        sums[2 * j + 1] = packed[j][8:16]
-
-    mine = lax.div(me, stride)
-    owner = lax.rem(me, stride) == 0
-    early = jnp.logical_and(owner, mine < EARLY)
-    late = jnp.logical_and(owner, mine >= EARLY)
-
-    def part_copy(j):
-        return pltpu.make_async_remote_copy(
-            src_ref=sums.at[j], dst_ref=parts.at[me], send_sem=s_send.at[j], recv_sem=s_recv,
-            device_id=device(j * stride), device_id_type=MESH)
-
-    def send_parts(low, high):
-        def step(j, carry):
-            @pl.when(j * stride != me)
-            def _():
-                part_copy(j).start()
-            return carry
-
-        lax.fori_loop(low, high, step, 0)
-
-    def total_copy(to, sem):
-        return pltpu.make_async_remote_copy(
-            src_ref=total.at[mine], dst_ref=total.at[mine], send_sem=t_send, recv_sem=t_recv.at[sem],
-            device_id=device(to), device_id_type=MESH)
-
-    def add_up(sem):
-        pltpu.make_async_copy(parts.at[pl.ds(0, count - 1)], parts.at[pl.ds(0, count - 1)], s_recv).wait()
-        parts[me] = sums[mine]
-        total[mine] = jnp.sum(parts[...], axis=0)
-
-        def step(k, carry):
-            total_copy(lax.rem(me + k, count), sem).start()
-            return carry
-
-        lax.fori_loop(1, count, step, 0)
-
-    def take(sem, tiles, is_mine):
-        def wait(n):
-            pltpu.make_async_copy(total.at[pl.ds(0, n)], total.at[pl.ds(0, n)], t_recv.at[sem]).wait()
-
-        @pl.when(is_mine)
-        def _():
-            wait(tiles - 1)
-
-        @pl.when(jnp.logical_not(is_mine))
-        def _():
-            wait(tiles)
-
-    send_parts(0, EARLY)
+    row2 = as_row(jnp.sum(grad_sum, axis=1, keepdims=True), 32)
+    packed.append(jnp.where(lax.broadcasted_iota(jnp.int32, (16, 128), 0) == 0, row2, 0.0))
+    sums[...] = jnp.concatenate(packed, axis=0).reshape(sums.shape)
+
+    class Step:
+        def __init__(self, src, dst, slot, target, size, send, recv):
+            def copy(k):
+                return pltpu.make_async_remote_copy(
+                    src_ref=src(k), dst_ref=dst.at[slot], send_sem=send, recv_sem=recv,
+                    device_id=target(k), device_id_type=MESH)
+
+            self.copy, self.all, self.size, self.send, self.recv = copy, dst, size, send, recv
+
+        def start(self):
+            def step(k, carry):
+                self.copy(k).start()
+                return carry
+
+            lax.fori_loop(1, self.size, step, 0)
+
+        def wait(self, sem):
+            others = self.all.at[pl.ds(0, self.size - 1)]
+            pltpu.make_async_copy(others, others, sem).wait()
+
+        def receive(self):
+            self.wait(self.recv)
+
+        def finish(self):
+            self.wait(self.send)
+
+    spread_out = Step(lambda k: sums.at[lax.rem(sp + k, ns)], near, sp, beside, ns, near_sem.at[0], near_sem.at[1])
+    sum_far = Step(lambda k: far.at[dp], far, dp, across, nd, far_sem.at[0], far_sem.at[1])
+    collect = Step(lambda k: total.at[sp], total, sp, beside, ns, near_sem.at[2], near_sem.at[3])
+    small_near = Step(lambda k: late_near.at[sp], late_near, sp, beside, ns, near_sem.at[4], near_sem.at[5])
+    small_far = Step(lambda k: late_far.at[dp], late_far, dp, across, nd, far_sem.at[2], far_sem.at[3])
+    spread_out.start()
+    near[sp] = sums[sp]
 
     res = (out_sum * 0.125).astype(BF16)
     res = jnp.concatenate([res[:, 0:128], res[:, 128:256]], axis=0)
@@ -357,6 +349,9 @@
     spread(ghalo[128:256], 32, gradx, 1536)
     back = back + dot(wback[:, 0:512], gradx[0:512]) + dot(wback[:, 1536:2048], gradx[1536:2048])
 
+    spread_out.receive()
+    far[dp] = jnp.sum(near[...], axis=0)
+    sum_far.start()
     prod = jnp.zeros((432, 256), F32)
     bias_sum = jnp.zeros((16, 256), F32)
     for i in range(4):
@@ -392,48 +387,35 @@
         blk = jnp.where(lanes(16) // 16 == g, fold_b[14 * g : 14 * g + 16, :], blk)
     at = lax.broadcasted_iota(jnp.int32, (16, 128), 0)
     row1 = as_row(jnp.sum(bias_sum, axis=1, keepdims=True), 16)
-    row2 = as_row(jnp.sum(grad_sum, axis=1, keepdims=True), 32)
-    blk = jnp.where(at == 14, row1, jnp.where(at == 15, row2, blk))
-    sums[EARLY] = blk[0:8]
-    sums[EARLY + 1] = blk[8:16]
-    send_parts(EARLY, TILES)
-
-    @pl.when(early)
-    def _():
-        add_up(0)
-
-    @pl.when(late)
-    def _():
-        add_up(1)
-
-    take(0, EARLY, early)
-    take(1, TILES - EARLY, late)
+    late_near[sp] = jnp.where(at == 14, row1, jnp.where(at == 15, 0.0, blk))
+    small_near.start()
+    small_near.receive()
+    late_far[dp] = jnp.sum(late_near[...], axis=0)
+    small_far.start()
+    sum_far.receive()
+    total[sp] = jnp.sum(far[...], axis=0)
+    collect.start()
+    collect.receive()
+    small_far.receive()
+    late[...] = jnp.sum(late_far[...], axis=0)
+
     ex_field.finish()
     ex_pool.finish()
     ex_grad.finish()
 
-    def sent(j, carry):
-        @pl.when(j * stride != me)
-        def _():
-            part_copy(j).wait_send()
-        return carry
-
-    lax.fori_loop(0, TILES, sent, 0)
-
-    @pl.when(owner)
-    def _():
-        pltpu.make_async_copy(parts.at[pl.ds(0, count - 1)], parts.at[pl.ds(0, count - 1)], t_send).wait()
-
-
-def unpack(res, total, out, gw2, gw1, gb1, gb2, rows):
+    for step in (spread_out, sum_far, collect, small_near, small_far):
+        step.finish()
+
+
+def unpack(res, total, late, out, gw2, gw1, gb1, gb2, rows):
     out[...] = res[...]
     for g in range(4):
         n = 112 if g < 3 else 96
-        blk = total[0 : n // 8].reshape(n, 128)
+        blk = total[0:n]
         if g:
             blk = pltpu.roll(blk, 128 - 32 * g, 1)
         gw2[112 * g : 112 * g + n] = blk[:, 0:32]
-    blk = jnp.concatenate([total[EARLY], total[EARLY + 1]], axis=0)
+    blk = late[...]
     for g in range(8):
         n = 14 if g < 7 else 10
         turned = pltpu.roll(blk, 128 - 16 * g, 1) if g else blk
@@ -441,7 +423,7 @@
     for k in range(27):
         gw1[k] = rows[4 * k : 4 * k + 4, 0:16]
     gb1[...] = blk[14:15, 0:16]
-    gb2[...] = blk[15:16, 0:32]
+    gb2[...] = total[112:113, 0:32]
 
 
 def tables():
@@ -466,7 +448,7 @@
 
 
 def shards(nd, ns, volume, cotangent, w_first, b_first, w_second, b_second):
-    count = nd * ns
+    each = EARLY // ns
     w1 = jnp.transpose(w_first, (2, 3, 4, 1, 0)).reshape(27, 4, 16)
     w2 = jnp.transpose(w_second, (2, 3, 4, 1, 0)).reshape(432, 32)
     vm = pl.BlockSpec(memory_space=pltpu.VMEM)
@@ -475,14 +457,15 @@
         volume.reshape(128, 512), cotangent.reshape(64, 128), w1, b_first.reshape(1, 16), w2,
         b_second.reshape(1, 32), *tables(),
     ]
-    out, total = pl.pallas_call(
+    out, total, late = pl.pallas_call(
         functools.partial(kernel, nd, ns),
         out_shape=[
             jax.ShapeDtypeStruct((64, 128), BF16),
-            jax.ShapeDtypeStruct((TILES, 8, 128), F32),
+            jax.ShapeDtypeStruct((ns, each, 128), F32),
+            jax.ShapeDtypeStruct((LATE, 128), F32),
         ],
         in_specs=[pl.BlockSpec(memory_space=pltpu.HBM)] * INPUTS,
-        out_specs=[vm] * 2,
+        out_specs=[vm] * 3,
         scratch_shapes=[pltpu.VMEM(a.shape, a.dtype) for a in operands]
         + [
             pltpu.VMEM((864, 256), BF16),
@@ -500,15 +483,16 @@
             pltpu.VMEM((9, 24, 128), F32),
             pltpu.VMEM((120, 128), F32),
             pltpu.VMEM((144, 16), F32),
-            pltpu.VMEM((TILES, 8, 128), F32),
-            pltpu.VMEM((count, 8, 128), F32),
+            pltpu.VMEM((ns, each, 128), F32),
+            pltpu.VMEM((ns, each, 128), F32),
+            pltpu.VMEM((nd, each, 128), F32),
+            pltpu.VMEM((ns, LATE, 128), F32),
+            pltpu.VMEM((nd, LATE, 128), F32),
             dma((INPUTS,)),
             dma((6,)),
             dma((6,)),
-            dma((TILES,)),
-            dma,
-            dma,
-            dma((2,)),
+            dma((6,)),
+            dma((4,)),
         ],
         compiler_params=pltpu.CompilerParams(
             collective_id=0, has_side_effects=True, vmem_limit_bytes=62 * 1024 * 1024),
@@ -523,11 +507,11 @@
             jax.ShapeDtypeStruct((1, 16), F32),
             jax.ShapeDtypeStruct((1, 32), F32),
         ],
-        in_specs=[vm] * 2,
+        in_specs=[vm] * 3,
         out_specs=[vm] * 5,
         scratch_shapes=[pltpu.VMEM((112, 128), F32)],
 
-    )(out, total)
+    )(out, total.reshape(EARLY, 128), late)
     grad_w1 = jnp.transpose(gw1.reshape(3, 3, 3, 4, 16), (4, 3, 0, 1, 2))
     grad_w2 = jnp.transpose(gw2.reshape(3, 3, 3, 16, 32), (4, 3, 0, 1, 2))
     return out.reshape(1, 32, 1, 2, 128), grad_w1, gb1.reshape(16), grad_w2, gb2.reshape(32)

time: 29.8 us -> 26.3 us (0.88)
  Pallas kernels: 28.9 us -> 25.5 us
    pallas_call x1, Pallas kernels: 27.2 us -> 23.8 us  [shards(): pl.pallas_call(functools.partial(kernel, nd, ns), out_shape=[jax.ShapeDty...]
where the time goes in v2:
time: 26.3 us; the launch traced here: 26.1 us
  Pallas kernels  25.5 us (97%)
  between operations  0.64 us (2%)
    pallas_call x1, Pallas kernels, shards(): pl.pallas_call(functools.partial(kernel, nd, ns), out_shape=[jax.ShapeDty...  23.8 us
    pallas_call x1, Pallas kernels, shards(): pl.pallas_call(unpack, out_shape=[jax.ShapeDtypeStruct((64, 128), BF16),...  1.67 us

profile of v2, /device:TPU:0, one launch (start us, length us, event | category | flops | bytes accessed | tf_op | source)
XLA Modules:
  0.0 26.1 jit_solution(7417220677853518406)
XLA Ops:
  0.6 23.8 %shard_map.146 = (bf16[64,128]{1,0:T(8,128)(2,1)}, f32[4,32,128]{2,1,0:T(8,128)}, f32[16,128]{1,0:T(8,128)}) custom-call(bf16[128,512]{1,0:T(8,128)(2,1)} %bitcast.24, bf16[64,128]{1,0:T(8,128)(2,1)} %bitcast.28, bf16[27,4,16]{2,1,0:T(4,128)(2,1)} %bitcast.27, f32[1,16]{1,0:T(1,128)} %bitcast.30, bf16[432,32]{1,0:T(8,128)(2,1)} %bitcast.25, ...), custom_call_target="tpu_custom_call" | custom-call | flops 1000000000 | bytes 2000000 | tf_op jit(solution)/shard_map/pallas_call | solution.py:460
  24.5 1.7 %shard_map.147 = (bf16[64,128]{1,0:T(8,128)(2,1)}, f32[432,32]{1,0:T(8,128)}, f32[27,4,16]{2,1,0:T(4,128)}, f32[1,16]{1,0:T(1,128)}, f32[1,32]{1,0:T(1,128)}) custom-call(bf16[64,128]{1,0:T(8,128)(2,1)} %get-tuple-element.13.res, f32[128,128]{1,0:T(8,128)} %bitcast.22, f32[16,128]{1,0:T(8,128)} %get-tuple-element.15.late), custom_call_target="tpu_custom_call" | custom-call | tf_op jit(solution)/shard_map/pallas_call | solution.py:501
